TPU v7x, 32 devices: a whole 2x2x4 slice. The times are simulated.
32 devices in a mesh: groups: 2 (over y), age: 4 (over z), span: 2 (over x), blade: 2 (over core).
Axes of the slice: x: 2, y: 2, z: 4, core: 2. Of those that a mesh axis runs over, the one named last changes fastest.
Arguments:
- surface_mu: float32 [32, 4, 64, 128], P(('groups', 'age'), 'blade', None, 'span'), parts along dimension 0, may hold values from -6 to 6
- centroid_body: float32 [3, 4, 64, 128], P(None, 'blade', None, 'span'), may hold values from -0.04 to 1.01
- area_normal: float32 [3, 4, 64, 128], P(None, 'blade', None, 'span'), may hold values from -0.12 to 0.12
- te_body: float32 [3, 4, 128], P(None, 'blade', 'span'), may hold values from -0.04 to 1.01
- wake_state: float32 [4, 4, 64, 2, 128], P(None, 'blade', ('groups', 'age'), 'span'), parts along dimension 2, may hold values from -2 to 2
- pairs: int32 [4, 64, 2, 8], P('blade', ('groups', 'age'), 'span'), parts along dimension 1, may hold values from -1 to 71, as said below
- az_index: int32 [6], P('groups'), parts along dimension 0, may hold values from 0 to 15
- free_stream: float32 [6], P('groups'), parts along dimension 0, may hold values from -3 to 3
Outputs:
- wake_final: float32 [4, 4, 64, 2, 128], P(None, 'blade', ('groups', 'age'), 'span'), parts along dimension 2
- wake_velocity: float32 [3, 4, 64, 2, 128], P(None, 'blade', ('groups', 'age'), 'span'), parts along dimension 2
There are 2 independent parts, one for each index of `groups`. A program takes and returns all parts, laid end to end along the dimension named above; an argument that names none is the same for every part. Nothing has to cross between parts.
Inputs may be any that keep to these rules, and one draw needn't show every extreme that they name: Rows come in age blocks of 16 rows (8 tiles), spanwise panels in strips of 64. An entry v >= 0 of pairs[b, t, s, :] names tile v % 8 of age block t // 8 + v // 24 - 1 in strip s + (v // 8) % 3 - 1 of the same blade; -1 marks an empty slot. In each aligned block of 2 blades, one age block and one strip, at most 64 entries are not -1, and exactly 64 in one such block.
All inputs are finite; a program needn't handle non-finite values.
Results may differ from a plain program's by a relative error of at most 0.0003.
Values sent between devices are 32-bit elements; how exact they have to be, the bound alone decides.
A program may use at most 64 MiB of HBM per device.

v0:
```python
import math
import jax
import jax.numpy as jnp
from jax import lax
from jax.sharding import PartitionSpec as P

CB = 8
time_step = 0.05
near_core = 0.0025
far_core = 0.01
inv_four_pi = 0.25 / math.pi


def spread(shard, axis, root):
    mine = lax.axis_index(axis) == root
    return lax.psum(jnp.where(mine, shard, jnp.zeros_like(shard)), axis)


def with_halo(cells, sides, width):
    for axis, dim in sides:
        count = lax.axis_size(axis)
        ends = count - 1
        head = lax.slice_in_dim(cells, 0, width, axis=dim)
        tail = lax.slice_in_dim(cells, cells.shape[dim] - width, cells.shape[dim], axis=dim)
        cells = jnp.concatenate(
            [
                lax.ppermute(tail, axis, [(i, (i + 1) % count) for i in range(ends)]),
                cells,
                lax.ppermute(head, axis, [((i + 1) % count, i) for i in range(ends)]),
            ],
            axis=dim,
        )
    return cells


def shifted(value, axis, steps):
    count = lax.axis_size(axis)
    first, last = (max(0, -steps), min(count, count - steps))
    return lax.ppermute(value, axis, [(source, source + steps) for source in range(first, last)])


def rotate(vector, cosine, sine_val):
    return jnp.stack(
        [
            vector[0] * cosine - vector[1] * sine_val,
            vector[0] * sine_val + vector[1] * cosine,
            vector[2],
        ]
    )


def coarse_sum(values, block_size):
    shape = values.shape
    grouped = values.reshape(
        shape[:-2] + (shape[-2] // block_size, block_size, shape[-1] // block_size, block_size)
    )
    return jnp.sum(grouped, axis=(-3, -1))


def far_velocity(targets, centers, moments):
    separation = targets[:, :, None] - centers[:, None, :]
    dist_sq = jnp.sum(separation * separation, axis=0) + far_core
    inverse = 1.0 / jnp.sqrt(dist_sq)
    inverse_cube = inverse * inverse * inverse
    projection = jnp.sum(moments[:, None, :] * separation, axis=0)
    values = (
        3.0 * projection * inverse_cube * inverse * inverse * separation
        - moments[:, None, :] * inverse_cube
    )
    return inv_four_pi * jnp.sum(values, axis=2)


def near_velocity(targets, sources, strengths):
    separation = targets[:, :, None] - sources[:, None, :]
    dist_sq = jnp.sum(separation * separation, axis=0) + near_core
    weight = 1.0 / (dist_sq * jnp.sqrt(dist_sq))
    cross_prod = jnp.stack(
        [
            strengths[1][None, :] * separation[2] - strengths[2][None, :] * separation[1],
            strengths[2][None, :] * separation[0] - strengths[0][None, :] * separation[2],
            strengths[0][None, :] * separation[1] - strengths[1][None, :] * separation[0],
        ]
    )
    return inv_four_pi * jnp.sum(cross_prod * weight[None], axis=2)


def sheet_strength(pos_pad, mu_pad):
    pos_r = 0.5 * (pos_pad[:, :, 2:, 1:-1] - pos_pad[:, :, :-2, 1:-1])
    pos_s = 0.5 * (pos_pad[:, :, 1:-1, 2:] - pos_pad[:, :, 1:-1, :-2])
    mu_r = 0.5 * (mu_pad[:, 2:, 1:-1] - mu_pad[:, :-2, 1:-1])
    mu_s = 0.5 * (mu_pad[:, 1:-1, 2:] - mu_pad[:, 1:-1, :-2])
    return mu_s[None] * pos_r - mu_r[None] * pos_s


def grouped_map(kernel, operands):
    length = jax.tree.leaves(operands)[0].shape[0]
    turn_count = math.gcd(length, 16)
    shaped = jax.tree.map(
        lambda array: array.reshape((turn_count, length // turn_count) + array.shape[1:]), operands
    )
    result = lax.map(jax.vmap(kernel), shaped)
    return result.reshape((length,) + result.shape[2:])


def far_kernel(centers, moments):

    def apply_one(target_tile):
        return far_velocity(target_tile, centers, moments)

    return apply_one


def near_kernel(bundle):
    return near_velocity(bundle[0], bundle[1], bundle[2])


def on_device(
    surface_mu, centroid_body, area_normal, te_body, wake_state, pairs, az_index, free_stream
):
    az_dev, blade_group, chord_len, span_dev = surface_mu.shape
    tile_dev = wake_state.shape[2]
    lanes = wake_state.shape[4]
    rows_dev = tile_dev * lanes // span_dev
    slot_tile = pairs.shape[3]
    step_count = az_index.shape[0]
    age_count = lax.axis_size("age")
    span_count = lax.axis_size("span")
    blade_count = lax.axis_size("blade")
    age_pos = lax.axis_index("age")
    span_pos = lax.axis_index("span")
    blade_pos = lax.axis_index("blade")
    naz_total = az_dev * age_count
    blade_total = blade_group * blade_count
    tile_local = blade_group * tile_dev
    block_cells = chord_len // CB * (span_dev // CB)
    per_device = blade_group * block_cells
    column = jnp.arange(per_device * span_count * blade_count, dtype=jnp.int32)
    column_blade = (
        column // per_device % blade_count * blade_group + column % per_device // block_cells
    )
    column_frac = column_blade.astype(jnp.float32) / blade_total
    local_frac = (blade_pos * blade_group + jnp.arange(blade_group, dtype=jnp.int32)).astype(
        jnp.float32
    ) / blade_total
    center_local = (coarse_sum(centroid_body, CB) / (CB * CB)).reshape(3, per_device)
    center_all = lax.all_gather(center_local, ("span", "blade"), axis=1, tiled=True)
    sheet_grid = wake_state[:, :, :, 0, :].reshape(4, blade_group, rows_dev, span_dev)
    velocity = jnp.zeros((3, blade_group, tile_dev, lanes), jnp.float32)
    for step_num in range(step_count):
        azimuth = az_index[step_num]
        mu_now = lax.dynamic_index_in_dim(surface_mu, azimuth % az_dev, 0, keepdims=False)
        moment_local = coarse_sum(mu_now[None] * area_normal, CB).reshape(3, per_device)
        trailing_local = (mu_now[:, chord_len - 1, :] - mu_now[:, 0, :]).reshape(
            blade_group * span_dev
        )
        moment_local, trailing_local = (moment_local, trailing_local)
        moment_got, trailing = (
            spread(moment_local, "age", azimuth // az_dev),
            spread(trailing_local, "age", azimuth // az_dev),
        )
        moment_all = lax.all_gather(moment_got, ("span", "blade"), axis=1, tiled=True)
        turn_frac = azimuth.astype(jnp.float32) / naz_total
        source_angle = 2.0 * math.pi * (turn_frac + column_frac)
        source_cos = jnp.cos(source_angle)
        source_sin = jnp.sin(source_angle)
        centers = rotate(center_all, source_cos, source_sin)
        moments = rotate(moment_all, source_cos, source_sin)
        padded = with_halo(sheet_grid, (("age", 2), ("span", 3)), 1)
        pos_pad = padded[:3]
        top_rows = jnp.where(age_pos == 0, pos_pad[:, :, 1, :], pos_pad[:, :, 0, :])
        bottom_rows = jnp.where(
            age_pos == age_count - 1, pos_pad[:, :, -2, :], pos_pad[:, :, -1, :]
        )
        pos_pad = jnp.concatenate(
            [top_rows[:, :, None], pos_pad[:, :, 1:-1], bottom_rows[:, :, None]], 2
        )
        left_cols = jnp.where(span_pos == 0, pos_pad[..., 1], pos_pad[..., 0])
        right_cols = jnp.where(span_pos == span_count - 1, pos_pad[..., -2], pos_pad[..., -1])
        pos_pad = jnp.concatenate(
            [left_cols[..., None], pos_pad[..., 1:-1], right_cols[..., None]], 3
        )
        strength = sheet_strength(pos_pad, padded[3])
        pos_tiles = sheet_grid[:3].reshape(3, blade_group, tile_dev, lanes)
        str_tiles = strength.reshape(3, blade_group, tile_dev, lanes)
        targets = pos_tiles.reshape(3, tile_local, lanes).transpose(1, 0, 2)
        far_field = grouped_map(far_kernel(centers, moments), targets)
        blocks = jnp.concatenate([pos_tiles, str_tiles], 0).transpose(1, 2, 0, 3)[:, None, None]
        beside_all = with_halo(blocks, (("age", 1), ("span", 2)), 1)
        source_table = beside_all.reshape(blade_group, 9 * tile_dev, 6, lanes)
        pair_ids = pairs[:, :, 0, :]
        live_mask = pair_ids >= 0
        safe_ids = jnp.maximum(pair_ids, 0)
        picked = source_table[jnp.arange(blade_group, dtype=jnp.int32)[:, None, None], safe_ids]
        weights = live_mask.astype(jnp.float32)[:, :, :, None, None]
        sources = (
            picked[:, :, :, :3]
            .reshape(tile_local, slot_tile, 3, lanes)
            .transpose(0, 2, 1, 3)
            .reshape(tile_local, 3, slot_tile * lanes)
        )
        strengths = (
            (picked[:, :, :, 3:] * weights)
            .reshape(tile_local, slot_tile, 3, lanes)
            .transpose(0, 2, 1, 3)
            .reshape(tile_local, 3, slot_tile * lanes)
        )
        near_flat = grouped_map(near_kernel, (targets, sources, strengths))
        far_part = far_field.transpose(1, 0, 2).reshape(3, blade_group, tile_dev, lanes)
        near_part = near_flat.transpose(1, 0, 2).reshape(3, blade_group, tile_dev, lanes)
        velocity = free_stream[:, None, None, None] + far_part + near_part
        moved_pos = sheet_grid[:3] + time_step * velocity.reshape(
            3, blade_group, rows_dev, span_dev
        )
        moved_state = jnp.concatenate([moved_pos, sheet_grid[3:4]], 0)
        incoming = shifted(moved_state[:, :, -1, :], "age", 1)
        blade_angle = 2.0 * math.pi * (turn_frac + local_frac)
        te_pos = rotate(te_body, jnp.cos(blade_angle)[:, None], jnp.sin(blade_angle)[:, None])
        shed_row = jnp.concatenate([te_pos, trailing.reshape(1, blade_group, span_dev)], 0)
        incoming = jnp.where(age_pos == 0, shed_row, incoming)
        sheet_grid = jnp.concatenate([incoming[:, :, None, :], moved_state[:, :, :-1, :]], 2)
    final_tiles = sheet_grid.reshape(4, blade_group, tile_dev, lanes)
    return (final_tiles[:, :, :, None, :], velocity[:, :, :, None, :])


def solution(mesh):
    in_specs = (
        P(("groups", "age"), "blade", None, "span"),
        P(None, "blade", None, "span"),
        P(None, "blade", None, "span"),
        P(None, "blade", "span"),
        P(None, "blade", ("groups", "age"), "span", None),
        P("blade", ("groups", "age"), "span", None),
        P("groups"),
        P("groups"),
    )
    out_specs = (
        P(None, "blade", ("groups", "age"), "span", None),
        P(None, "blade", ("groups", "age"), "span", None),
    )
    return jax.shard_map(
        on_device, mesh=mesh, in_specs=in_specs, out_specs=out_specs, check_vma=False
    )
```

profile of v0, /device:TPU:0, one launch (start us, length us, event | category | flops | bytes accessed | tf_op | source)
XLA Modules:
  0.0 256.7 jit_solution(8771473071030211586)
XLA Ops:
  2.7 4.9 %collective-permute-start = (f32[4,2,1,64]{3,1,2,0:T(2,128)S(1)}, f32[4,2,1,64]{3,1,2,0:T(2,128)S(1)}, u32[]{:S(2)}, u32[]{:S(2)}) collective-permute-start(f32[4,2,1,64]{3,1,2,0:T(2,128)S(1)} %copy.303), channel_id=1, source_target_pairs={{0,4},{4,8},{8,12},{1,5},{5,9},{9,13},{2,6},{6,10},{10,14},{3,7},{... | collective-permute-start | bytes 6152 | tf_op jit(solution)/shard_map/ppermute | solution.py:27
  26.2 13.3 %all-reduce = (f32[3,128]{1,0:T(4,128)S(1)}, f32[1,2,64]{2,1,0:T(2,128)S(1)}, f32[3,128]{1,0:T(4,128)S(1)}, f32[1,2,64]{2,1,0:T(2,128)S(1)}, f32[3,128]{1,0:T(4,128)S(1)}, /*index=5*/f32[1,2,64]{2,1,0:T(2,128)S(1)}) all-reduce(f32[3,128]{1,0:T(4,128)S(1)} %select_n.377, ...), channel_id=1, replica_groups=mesh['groups'=2,'age'=4,'span'=2,'blade'=2] {'age'}, use_global_device_ids=true, to_apply=%region_5.6 | all-reduce | flops 1536 | bytes 12288 | tf_op jit(solution)/shard_map/psum | solution.py:16
  39.6 5.2 %all_gather.12 = f32[3,512]{1,0:T(4,128)S(1)} all-gather(f32[3,128]{1,0:T(4,128)S(1)} %get-tuple-element.344), channel_id=1, replica_groups=mesh['groups'=2,'age'=4,'span'=2,'blade'=2] {'span','blade'}, dimensions={1}, use_global_device_ids=true | all-gather | bytes 7680 | tf_op jit(solution)/shard_map/all_gather | solution.py:161
  45.5 5.2 %all_gather.13 = f32[3,512]{1,0:T(4,128)S(1)} all-gather(f32[3,128]{1,0:T(4,128)S(1)} %div.142), channel_id=1, replica_groups=mesh['groups'=2,'age'=4,'span'=2,'blade'=2] {'span','blade'}, dimensions={1}, use_global_device_ids=true | all-gather | bytes 7680 | tf_op jit(solution)/shard_map/all_gather | solution.py:146
  51.0 9.9 %while.60 = (s32[]{:T(128)}, f32[16,1,3,128]{3,2,1,0:T(4,128)S(1)}, f32[3,512]{1,0:T(4,128)S(1)}, f32[16,1,3,128]{3,2,1,0:T(4,128)S(1)}, f32[3,512]{1,0:T(4,128)S(1)}, /*index=5*/s32[]{:T(128)}) while((s32[]{:T(128)}, f32[16,1,3,128]{3,2,1,0:T(4,128)S(1)}, f32[3,512]{1,0:T(4,128)S(1)}, f32[16,1,3,128]{3,2,1,0:T(4,128)S(1)}, ...), condition=%wide.region_10.11_spmd, body=%wide.region_6.10_spmd.sunk | while | flops 2293762 | bytes 2133589 | solution.py:101
  60.9 5.2 %all_gather.14 = f32[3,512]{1,0:T(4,128)S(1)} all-gather(f32[3,128]{1,0:T(4,128)S(1)} %get-tuple-element.346), channel_id=1, replica_groups=mesh['groups'=2,'age'=4,'span'=2,'blade'=2] {'span','blade'}, dimensions={1}, use_global_device_ids=true | all-gather | bytes 7680 | tf_op jit(solution)/shard_map/all_gather | solution.py:161
  68.5 4.5 %collective-permute-start.2 = (f32[4,2,18,1]{3,1,2,0:T(2,128)S(1)}, f32[4,2,18,1]{3,1,2,0:T(2,128)S(1)}, u32[]{:S(2)}, u32[]{:S(2)}) collective-permute-start(f32[4,2,18,1]{3,1,2,0:T(2,128)S(1)} %get-tuple-element.398), channel_id=1, source_target_pairs={{0,2},{1,3},{4,6},{5,7},{8,10},{9,11},{12,14},{13,15},{16,18},{17,... | collective-permute-start | bytes 1736 | tf_op jit(solution)/shard_map/ppermute | solution.py:27
  77.7 4.5 %collective-permute-start.4 = (f32[2,1,1,8,6,128]{5,3,0,4,2,1:T(8,128)S(1)}, f32[2,1,1,8,6,128]{5,3,0,4,2,1:T(8,128)S(1)}, u32[]{:S(2)}, u32[]{:S(2)}) collective-permute-start(f32[2,1,1,8,6,128]{5,3,0,4,2,1:T(8,128)S(1)} %maximum_bitcast_fusion.3), channel_id=1, source_target_pairs={{0,4},{4,8},{8,12},{1,5},{5,9},{9,13},{2,6},{6,10},{10,14},{3,7},{... | collective-permute-start | bytes 147464 | tf_op jit(solution)/shard_map/ppermute | solution.py:27
  82.4 1.6 collective-permute-done.4
  85.3 4.6 %collective-permute-start.6 = (f32[2,3,1,8,6,128]{5,3,0,4,2,1:T(8,128)S(1)}, f32[2,3,1,8,6,128]{5,3,0,4,2,1:T(8,128)S(1)}, u32[]{:S(2)}, u32[]{:S(2)}) collective-permute-start(f32[2,3,1,8,6,128]{5,3,0,4,2,1:T(8,128)S(1)} %pad_maximum_fusion.3), channel_id=1, source_target_pairs={{0,2},{1,3},{4,6},{5,7},{8,10},{9,11},{12,14},{13,15},{16,18},{17,... | collective-permute-start | bytes 442376 | tf_op jit(solution)/shard_map/ppermute | solution.py:27
  94.0 19.9 %while.61 = (s32[]{:T(128)}, f32[16,1,3,128]{3,2,1,0:T(4,128)S(1)}, f32[16,1,3,1024]{3,0,2,1:T(8,128)S(1)}, f32[16,1,3,128]{3,2,1,0:T(4,128)S(1)}, f32[16,1,3,1024]{3,0,2,1:T(8,128)S(1)}, /*index=5*/s32[]{:T(128)}) while((s32[]{:T(128)}, f32[16,1,3,128]{3,2,1,0:T(4,128)S(1)}, f32[16,1,3,1024]{3,0,2,1:T(8,128)S(1)}, ...), condition=%wide.region_14.15_spmd, body=%wide.region_11.14_spmd.sunk | while | flops 4587522 | bytes 8560217 | solution.py:101
  114.2 4.2 %collective-permute-start.8 = (f32[4,2,64]{2,1,0:T(2,128)S(1)}, f32[4,2,64]{2,1,0:T(2,128)S(1)}, u32[]{:S(2)}, u32[]{:S(2)}) collective-permute-start(f32[4,2,64]{2,1,0:T(2,128)S(1)} %get-tuple-element.403), channel_id=1, source_target_pairs={{0,4},{4,8},{8,12},{1,5},{5,9},{9,13},{2,6},{6,10},{10,14},{3,7},{... | collective-permute-start | bytes 6152 | tf_op jit(solution)/shard_map/ppermute | solution.py:39
  118.5 1.9 collective-permute-start.9
  121.8 4.1 %collective-permute-done.10 = f32[4,2,1,64]{3,1,0,2:T(2,128)S(1)} collective-permute-done((f32[4,2,1,64]{3,1,0,2:T(2,128)S(1)}, f32[4,2,1,64]{3,1,0,2:T(2,128)S(1)}, u32[]{:S(2)}, u32[]{:S(2)}) %collective-permute-start.10) | collective-permute-done | bytes 2080 | tf_op jit(solution)/shard_map/ppermute | solution.py:29
  127.5 4.5 %collective-permute-start.11 = (f32[4,2,18,1]{3,1,0,2:T(2,128)S(1)}, f32[4,2,18,1]{3,1,0,2:T(2,128)S(1)}, u32[]{:S(2)}, u32[]{:S(2)}) collective-permute-start(f32[4,2,18,1]{3,1,0,2:T(2,128)S(1)} %get-tuple-element.396), channel_id=1, source_target_pairs={{0,2},{1,3},{4,6},{5,7},{8,10},{9,11},{12,14},{13,15},{16,18},{17,... | collective-permute-start | bytes 1736 | tf_op jit(solution)/shard_map/ppermute | solution.py:27
  132.4 1.6 collective-permute-done.11
  136.7 4.5 %collective-permute-start.13 = (f32[2,1,1,8,6,128]{5,3,0,4,2,1:T(8,128)S(1)}, f32[2,1,1,8,6,128]{5,3,0,4,2,1:T(8,128)S(1)}, u32[]{:S(2)}, u32[]{:S(2)}) collective-permute-start(f32[2,1,1,8,6,128]{5,3,0,4,2,1:T(8,128)S(1)} %maximum_bitcast_fusion.4), channel_id=1, source_target_pairs={{0,4},{4,8},{8,12},{1,5},{5,9},{9,13},{2,6},{6,10},{10,14},{3,7},{... | collective-permute-start | bytes 147464 | tf_op jit(solution)/shard_map/ppermute | solution.py:27
  141.3 5.5 %all_gather.15 = f32[3,512]{1,0:T(4,128)S(1)} all-gather(f32[3,128]{1,0:T(4,128)S(1)} %get-tuple-element.348), channel_id=1, replica_groups=mesh['groups'=2,'age'=4,'span'=2,'blade'=2] {'span','blade'}, dimensions={1}, use_global_device_ids=true | all-gather | bytes 7680 | tf_op jit(solution)/shard_map/all_gather | solution.py:161
  148.3 4.7 %collective-permute-start.15 = (f32[2,3,1,8,6,128]{5,3,0,4,2,1:T(8,128)S(1)}, f32[2,3,1,8,6,128]{5,3,0,4,2,1:T(8,128)S(1)}, u32[]{:S(2)}, u32[]{:S(2)}) collective-permute-start(f32[2,3,1,8,6,128]{5,3,0,4,2,1:T(8,128)S(1)} %pad_maximum_fusion.4), channel_id=1, source_target_pairs={{0,2},{1,3},{4,6},{5,7},{8,10},{9,11},{12,14},{13,15},{16,18},{17,... | collective-permute-start | bytes 442376 | tf_op jit(solution)/shard_map/ppermute | solution.py:27
  153.1 9.9 %while.62 = (s32[]{:T(128)}, f32[16,1,3,128]{3,2,1,0:T(4,128)S(1)}, f32[3,512]{1,0:T(4,128)S(1)}, f32[16,1,3,128]{3,2,1,0:T(4,128)S(1)}, f32[3,512]{1,0:T(4,128)S(1)}, /*index=5*/s32[]{:T(128)}) while((s32[]{:T(128)}, f32[16,1,3,128]{3,2,1,0:T(4,128)S(1)}, f32[3,512]{1,0:T(4,128)S(1)}, f32[16,1,3,128]{3,2,1,0:T(4,128)S(1)}, ...), condition=%wide.region_21.22_spmd, body=%wide.region_17.21_spmd.sunk | while | flops 2293762 | bytes 2133589 | solution.py:101
  164.6 19.9 %while.63 = (s32[]{:T(128)}, f32[16,1,3,128]{3,2,1,0:T(4,128)S(1)}, f32[16,1,3,1024]{3,0,2,1:T(8,128)S(1)}, f32[16,1,3,128]{3,2,1,0:T(4,128)S(1)}, f32[16,1,3,1024]{3,0,2,1:T(8,128)S(1)}, /*index=5*/s32[]{:T(128)}) while((s32[]{:T(128)}, f32[16,1,3,128]{3,2,1,0:T(4,128)S(1)}, f32[16,1,3,1024]{3,0,2,1:T(8,128)S(1)}, ...), condition=%wide.region_25.26_spmd, body=%wide.region_22.25_spmd.sunk | while | flops 4587522 | bytes 8560217 | solution.py:101
  184.8 3.5 %collective-permute-start.17 = (f32[4,2,64]{2,1,0:T(2,128)S(1)}, f32[4,2,64]{2,1,0:T(2,128)S(1)}, u32[]{:S(2)}, u32[]{:S(2)}) collective-permute-start(f32[4,2,64]{2,1,0:T(2,128)S(1)} %get-tuple-element.401), channel_id=1, source_target_pairs={{0,4},{4,8},{8,12},{1,5},{5,9},{9,13},{2,6},{6,10},{10,14},{3,7},{... | collective-permute-start | bytes 6152 | tf_op jit(solution)/shard_map/ppermute | solution.py:39
  188.3 1.9 collective-permute-start.18
  191.6 4.2 %collective-permute-done.19 = f32[4,2,1,64]{3,1,2,0:T(2,128)S(1)} collective-permute-done((f32[4,2,1,64]{3,1,2,0:T(2,128)S(1)}, f32[4,2,1,64]{3,1,2,0:T(2,128)S(1)}, u32[]{:S(2)}, u32[]{:S(2)}) %collective-permute-start.19) | collective-permute-done | bytes 2080 | tf_op jit(solution)/shard_map/ppermute | solution.py:29
  197.3 4.5 %collective-permute-start.20 = (f32[4,2,18,1]{3,1,2,0:T(2,128)S(1)}, f32[4,2,18,1]{3,1,2,0:T(2,128)S(1)}, u32[]{:S(2)}, u32[]{:S(2)}) collective-permute-start(f32[4,2,18,1]{3,1,2,0:T(2,128)S(1)} %get-tuple-element.394), channel_id=1, source_target_pairs={{0,2},{1,3},{4,6},{5,7},{8,10},{9,11},{12,14},{13,15},{16,18},{17,... | collective-permute-start | bytes 1736 | tf_op jit(solution)/shard_map/ppermute | solution.py:27
  202.2 1.6 collective-permute-done.20
  206.6 4.5 %collective-permute-start.22 = (f32[2,1,1,8,6,128]{5,3,0,4,2,1:T(8,128)S(1)}, f32[2,1,1,8,6,128]{5,3,0,4,2,1:T(8,128)S(1)}, u32[]{:S(2)}, u32[]{:S(2)}) collective-permute-start(f32[2,1,1,8,6,128]{5,3,0,4,2,1:T(8,128)S(1)} %maximum_bitcast_fusion.5), channel_id=1, source_target_pairs={{0,4},{4,8},{8,12},{1,5},{5,9},{9,13},{2,6},{6,10},{10,14},{3,7},{... | collective-permute-start | bytes 147464 | tf_op jit(solution)/shard_map/ppermute | solution.py:27
  211.3 1.6 collective-permute-done.22
  214.2 4.6 %collective-permute-start.24 = (f32[2,3,1,8,6,128]{5,3,0,4,2,1:T(8,128)S(1)}, f32[2,3,1,8,6,128]{5,3,0,4,2,1:T(8,128)S(1)}, u32[]{:S(2)}, u32[]{:S(2)}) collective-permute-start(f32[2,3,1,8,6,128]{5,3,0,4,2,1:T(8,128)S(1)} %pad_maximum_fusion.5), channel_id=1, source_target_pairs={{0,2},{1,3},{4,6},{5,7},{8,10},{9,11},{12,14},{13,15},{16,18},{17,... | collective-permute-start | bytes 442376 | tf_op jit(solution)/shard_map/ppermute | solution.py:27
  218.8 9.9 %while.64 = (s32[]{:T(128)}, f32[16,1,3,128]{3,2,1,0:T(4,128)S(1)}, f32[3,512]{1,0:T(4,128)S(1)}, f32[16,1,3,128]{3,2,1,0:T(4,128)S(1)}, f32[3,512]{1,0:T(4,128)S(1)}, /*index=5*/s32[]{:T(128)}) while((s32[]{:T(128)}, f32[16,1,3,128]{3,2,1,0:T(4,128)S(1)}, f32[3,512]{1,0:T(4,128)S(1)}, f32[16,1,3,128]{3,2,1,0:T(4,128)S(1)}, ...), condition=%wide.region_32.33_spmd, body=%wide.region_28.32_spmd.sunk | while | flops 2293762 | bytes 2133589 | solution.py:101
  230.3 19.9 %while.65 = (s32[]{:T(128)}, f32[16,1,3,128]{3,2,1,0:T(4,128)S(1)}, f32[16,1,3,1024]{3,0,2,1:T(8,128)S(1)}, f32[16,1,3,128]{3,2,1,0:T(4,128)S(1)}, f32[16,1,3,1024]{3,0,2,1:T(8,128)S(1)}, /*index=5*/s32[]{:T(128)}) while((s32[]{:T(128)}, f32[16,1,3,128]{3,2,1,0:T(4,128)S(1)}, f32[16,1,3,1024]{3,0,2,1:T(8,128)S(1)}, ...), condition=%wide.region_36.37_spmd, body=%wide.region_33.36_spmd.sunk | while | flops 4587522 | bytes 8560217 | solution.py:101
  250.4 4.2 %collective-permute-start.26 = (f32[4,2,64]{2,1,0:T(2,128)S(1)}, f32[4,2,64]{2,1,0:T(2,128)S(1)}, u32[]{:S(2)}, u32[]{:S(2)}) collective-permute-start(f32[4,2,64]{2,1,0:T(2,128)S(1)} %bitcast.385), channel_id=1, source_target_pairs={{0,4},{4,8},{8,12},{1,5},{5,9},{9,13},{2,6},{6,10},{10,14},{3,7},{... | collective-permute-start | bytes 6152 | tf_op jit(solution)/shard_map/ppermute | solution.py:39
  (973 shorter events, 128.6 us)
Async XLA Ops:
  2.7 64.2 %collective-permute-start = (f32[4,2,1,64]{3,1,2,0:T(2,128)S(1)}, f32[4,2,1,64]{3,1,2,0:T(2,128)S(1)}, u32[]{:S(2)}, u32[]{:S(2)}) collective-permute-start(f32[4,2,1,64]{3,1,2,0:T(2,128)S(1)} %copy.303), channel_id=1, source_target_pairs={{0,4},{4,8},{8,12},{1,5},{5,9},{9,13},{2,6},{6,10},{10,14},{3,7},{... | collective-permute-start | bytes 6152 | tf_op jit(solution)/shard_map/ppermute | solution.py:27
  7.7 59.3 %collective-permute-start.1 = (f32[4,2,1,64]{3,1,2,0:T(2,128)S(1)}, f32[4,2,1,64]{3,1,2,0:T(2,128)S(1)}, u32[]{:S(2)}, u32[]{:S(2)}) collective-permute-start(f32[4,2,1,64]{3,1,2,0:T(2,128)S(1)} %copy.304), channel_id=1, source_target_pairs={{4,0},{8,4},{12,8},{5,1},{9,5},{13,9},{6,2},{10,6},{14,10},{7,3},{... | collective-permute-start | bytes 6152 | tf_op jit(solution)/shard_map/ppermute | solution.py:29
  25.5 19.3 %copy-start = (f32[3,2,64,64]{3,2,1,0:T(8,128)S(1)}, f32[3,2,64,64]{3,2,1,0:T(8,128)}, u32[]{:S(2)}) copy-start(f32[3,2,64,64]{3,2,1,0:T(8,128)} %param.21) | copy-start | bytes 294916
  67.2 6.4 %collective-permute-start.3 = (f32[4,2,18,1]{3,1,2,0:T(2,128)S(1)}, f32[4,2,18,1]{3,1,2,0:T(2,128)S(1)}, u32[]{:S(2)}, u32[]{:S(2)}) collective-permute-start(f32[4,2,18,1]{3,1,2,0:T(2,128)S(1)} %get-tuple-element.399), channel_id=1, source_target_pairs={{2,0},{3,1},{6,4},{7,5},{10,8},{11,9},{14,12},{15,13},{18,16},{19,... | collective-permute-start | bytes 1736 | tf_op jit(solution)/shard_map/ppermute | solution.py:29
  68.5 6.5 %collective-permute-start.2 = (f32[4,2,18,1]{3,1,2,0:T(2,128)S(1)}, f32[4,2,18,1]{3,1,2,0:T(2,128)S(1)}, u32[]{:S(2)}, u32[]{:S(2)}) collective-permute-start(f32[4,2,18,1]{3,1,2,0:T(2,128)S(1)} %get-tuple-element.398), channel_id=1, source_target_pairs={{0,2},{1,3},{4,6},{5,7},{8,10},{9,11},{12,14},{13,15},{16,18},{17,... | collective-permute-start | bytes 1736 | tf_op jit(solution)/shard_map/ppermute | solution.py:27
  76.4 6.0 %collective-permute-start.5 = (f32[2,1,1,8,6,128]{5,3,0,4,2,1:T(8,128)S(1)}, f32[2,1,1,8,6,128]{5,3,0,4,2,1:T(8,128)S(1)}, u32[]{:S(2)}, u32[]{:S(2)}) collective-permute-start(f32[2,1,1,8,6,128]{5,3,0,4,2,1:T(8,128)S(1)} %maximum_bitcast_fusion.3), channel_id=1, source_target_pairs={{4,0},{8,4},{12,8},{5,1},{9,5},{13,9},{6,2},{10,6},{14,10},{7,3},{... | collective-permute-start | bytes 147464 | tf_op jit(solution)/shard_map/ppermute | solution.py:29
  77.7 6.3 %collective-permute-start.4 = (f32[2,1,1,8,6,128]{5,3,0,4,2,1:T(8,128)S(1)}, f32[2,1,1,8,6,128]{5,3,0,4,2,1:T(8,128)S(1)}, u32[]{:S(2)}, u32[]{:S(2)}) collective-permute-start(f32[2,1,1,8,6,128]{5,3,0,4,2,1:T(8,128)S(1)} %maximum_bitcast_fusion.3), channel_id=1, source_target_pairs={{0,4},{4,8},{8,12},{1,5},{5,9},{9,13},{2,6},{6,10},{10,14},{3,7},{... | collective-permute-start | bytes 147464 | tf_op jit(solution)/shard_map/ppermute | solution.py:27
  84.0 7.0 %collective-permute-start.7 = (f32[2,3,1,8,6,128]{5,3,0,4,2,1:T(8,128)S(1)}, f32[2,3,1,8,6,128]{5,3,0,4,2,1:T(8,128)S(1)}, u32[]{:S(2)}, u32[]{:S(2)}) collective-permute-start(f32[2,3,1,8,6,128]{5,3,0,4,2,1:T(8,128)S(1)} %pad_maximum_fusion.3), channel_id=1, source_target_pairs={{2,0},{3,1},{6,4},{7,5},{10,8},{11,9},{14,12},{15,13},{18,16},{19,... | collective-permute-start | bytes 442376 | tf_op jit(solution)/shard_map/ppermute | solution.py:29
  85.3 7.2 %collective-permute-start.6 = (f32[2,3,1,8,6,128]{5,3,0,4,2,1:T(8,128)S(1)}, f32[2,3,1,8,6,128]{5,3,0,4,2,1:T(8,128)S(1)}, u32[]{:S(2)}, u32[]{:S(2)}) collective-permute-start(f32[2,3,1,8,6,128]{5,3,0,4,2,1:T(8,128)S(1)} %pad_maximum_fusion.3), channel_id=1, source_target_pairs={{0,2},{1,3},{4,6},{5,7},{8,10},{9,11},{12,14},{13,15},{16,18},{17,... | collective-permute-start | bytes 442376 | tf_op jit(solution)/shard_map/ppermute | solution.py:27
  94.0 20.0 %copy-start.1 = (f32[3]{0:T(128)S(1)}, f32[3]{0:T(128)}, u32[]{:S(2)}) copy-start(f32[3]{0:T(128)} %param.27) | copy-start | bytes 40
  94.0 24.4 %copy-start.2 = (f32[3,2,64]{2,1,0:T(2,128)S(1)}, f32[3,2,64]{2,1,0:T(2,128)}, u32[]{:S(2)}) copy-start(f32[3,2,64]{2,1,0:T(2,128)} %param.23) | copy-start | bytes 4612
  114.2 6.3 %collective-permute-start.8 = (f32[4,2,64]{2,1,0:T(2,128)S(1)}, f32[4,2,64]{2,1,0:T(2,128)S(1)}, u32[]{:S(2)}, u32[]{:S(2)}) collective-permute-start(f32[4,2,64]{2,1,0:T(2,128)S(1)} %get-tuple-element.403), channel_id=1, source_target_pairs={{0,4},{4,8},{8,12},{1,5},{5,9},{9,13},{2,6},{6,10},{10,14},{3,7},{... | collective-permute-start | bytes 6152 | tf_op jit(solution)/shard_map/ppermute | solution.py:39
  118.5 3.3 %collective-permute-start.9 = (f32[4,2,1,64]{3,1,0,2:T(2,128)S(1)}, f32[4,2,1,64]{3,1,0,2:T(2,128)S(1)}, u32[]{:S(2)}, u32[]{:S(2)}) collective-permute-start(f32[4,2,1,64]{3,1,0,2:T(2,128)S(1)} %get-tuple-element.402), channel_id=1, source_target_pairs={{0,4},{4,8},{8,12},{1,5},{5,9},{9,13},{2,6},{6,10},{10,14},{3,7},{... | collective-permute-start | bytes 6152 | tf_op jit(solution)/shard_map/ppermute | solution.py:27
  120.5 5.5 %collective-permute-start.10 = (f32[4,2,1,64]{3,1,0,2:T(2,128)S(1)}, f32[4,2,1,64]{3,1,0,2:T(2,128)S(1)}, u32[]{:S(2)}, u32[]{:S(2)}) collective-permute-start(f32[4,2,1,64]{3,1,0,2:T(2,128)S(1)} %fusion.57), channel_id=1, source_target_pairs={{4,0},{8,4},{12,8},{5,1},{9,5},{13,9},{6,2},{10,6},{14,10},{7,3},{... | collective-permute-start | bytes 6152 | tf_op jit(solution)/shard_map/ppermute | solution.py:29
  126.2 6.2 %collective-permute-start.12 = (f32[4,2,18,1]{3,1,0,2:T(2,128)S(1)}, f32[4,2,18,1]{3,1,0,2:T(2,128)S(1)}, u32[]{:S(2)}, u32[]{:S(2)}) collective-permute-start(f32[4,2,18,1]{3,1,0,2:T(2,128)S(1)} %get-tuple-element.397), channel_id=1, source_target_pairs={{2,0},{3,1},{6,4},{7,5},{10,8},{11,9},{14,12},{15,13},{18,16},{19,... | collective-permute-start | bytes 1736 | tf_op jit(solution)/shard_map/ppermute | solution.py:29
  127.5 6.5 %collective-permute-start.11 = (f32[4,2,18,1]{3,1,0,2:T(2,128)S(1)}, f32[4,2,18,1]{3,1,0,2:T(2,128)S(1)}, u32[]{:S(2)}, u32[]{:S(2)}) collective-permute-start(f32[4,2,18,1]{3,1,0,2:T(2,128)S(1)} %get-tuple-element.396), channel_id=1, source_target_pairs={{0,2},{1,3},{4,6},{5,7},{8,10},{9,11},{12,14},{13,15},{16,18},{17,... | collective-permute-start | bytes 1736 | tf_op jit(solution)/shard_map/ppermute | solution.py:27
  135.4 11.5 %collective-permute-start.14 = (f32[2,1,1,8,6,128]{5,3,0,4,2,1:T(8,128)S(1)}, f32[2,1,1,8,6,128]{5,3,0,4,2,1:T(8,128)S(1)}, u32[]{:S(2)}, u32[]{:S(2)}) collective-permute-start(f32[2,1,1,8,6,128]{5,3,0,4,2,1:T(8,128)S(1)} %maximum_bitcast_fusion.4), channel_id=1, source_target_pairs={{4,0},{8,4},{12,8},{5,1},{9,5},{13,9},{6,2},{10,6},{14,10},{7,3},{... | collective-permute-start | bytes 147464 | tf_op jit(solution)/shard_map/ppermute | solution.py:29
  136.7 10.2 %collective-permute-start.13 = (f32[2,1,1,8,6,128]{5,3,0,4,2,1:T(8,128)S(1)}, f32[2,1,1,8,6,128]{5,3,0,4,2,1:T(8,128)S(1)}, u32[]{:S(2)}, u32[]{:S(2)}) collective-permute-start(f32[2,1,1,8,6,128]{5,3,0,4,2,1:T(8,128)S(1)} %maximum_bitcast_fusion.4), channel_id=1, source_target_pairs={{0,4},{4,8},{8,12},{1,5},{5,9},{9,13},{2,6},{6,10},{10,14},{3,7},{... | collective-permute-start | bytes 147464 | tf_op jit(solution)/shard_map/ppermute | solution.py:27
  147.0 16.1 %collective-permute-start.16 = (f32[2,3,1,8,6,128]{5,3,0,4,2,1:T(8,128)S(1)}, f32[2,3,1,8,6,128]{5,3,0,4,2,1:T(8,128)S(1)}, u32[]{:S(2)}, u32[]{:S(2)}) collective-permute-start(f32[2,3,1,8,6,128]{5,3,0,4,2,1:T(8,128)S(1)} %pad_maximum_fusion.4), channel_id=1, source_target_pairs={{2,0},{3,1},{6,4},{7,5},{10,8},{11,9},{14,12},{15,13},{18,16},{19,... | collective-permute-start | bytes 442376 | tf_op jit(solution)/shard_map/ppermute | solution.py:29
  148.3 14.8 %collective-permute-start.15 = (f32[2,3,1,8,6,128]{5,3,0,4,2,1:T(8,128)S(1)}, f32[2,3,1,8,6,128]{5,3,0,4,2,1:T(8,128)S(1)}, u32[]{:S(2)}, u32[]{:S(2)}) collective-permute-start(f32[2,3,1,8,6,128]{5,3,0,4,2,1:T(8,128)S(1)} %pad_maximum_fusion.4), channel_id=1, source_target_pairs={{0,2},{1,3},{4,6},{5,7},{8,10},{9,11},{12,14},{13,15},{16,18},{17,... | collective-permute-start | bytes 442376 | tf_op jit(solution)/shard_map/ppermute | solution.py:27
  184.8 5.5 %collective-permute-start.17 = (f32[4,2,64]{2,1,0:T(2,128)S(1)}, f32[4,2,64]{2,1,0:T(2,128)S(1)}, u32[]{:S(2)}, u32[]{:S(2)}) collective-permute-start(f32[4,2,64]{2,1,0:T(2,128)S(1)} %get-tuple-element.401), channel_id=1, source_target_pairs={{0,4},{4,8},{8,12},{1,5},{5,9},{9,13},{2,6},{6,10},{10,14},{3,7},{... | collective-permute-start | bytes 6152 | tf_op jit(solution)/shard_map/ppermute | solution.py:39
  188.3 3.3 %collective-permute-start.18 = (f32[4,2,1,64]{3,1,0,2:T(2,128)S(1)}, f32[4,2,1,64]{3,1,0,2:T(2,128)S(1)}, u32[]{:S(2)}, u32[]{:S(2)}) collective-permute-start(f32[4,2,1,64]{3,1,0,2:T(2,128)S(1)} %get-tuple-element.400), channel_id=1, source_target_pairs={{0,4},{4,8},{8,12},{1,5},{5,9},{9,13},{2,6},{6,10},{10,14},{3,7},{... | collective-permute-start | bytes 6152 | tf_op jit(solution)/shard_map/ppermute | solution.py:27
  190.3 5.5 %collective-permute-start.19 = (f32[4,2,1,64]{3,1,2,0:T(2,128)S(1)}, f32[4,2,1,64]{3,1,2,0:T(2,128)S(1)}, u32[]{:S(2)}, u32[]{:S(2)}) collective-permute-start(f32[4,2,1,64]{3,1,2,0:T(2,128)S(1)} %fusion.89), channel_id=1, source_target_pairs={{4,0},{8,4},{12,8},{5,1},{9,5},{13,9},{6,2},{10,6},{14,10},{7,3},{... | collective-permute-start | bytes 6152 | tf_op jit(solution)/shard_map/ppermute | solution.py:29
  196.0 6.2 %collective-permute-start.21 = (f32[4,2,18,1]{3,1,2,0:T(2,128)S(1)}, f32[4,2,18,1]{3,1,2,0:T(2,128)S(1)}, u32[]{:S(2)}, u32[]{:S(2)}) collective-permute-start(f32[4,2,18,1]{3,1,2,0:T(2,128)S(1)} %get-tuple-element.395), channel_id=1, source_target_pairs={{2,0},{3,1},{6,4},{7,5},{10,8},{11,9},{14,12},{15,13},{18,16},{19,... | collective-permute-start | bytes 1736 | tf_op jit(solution)/shard_map/ppermute | solution.py:29
  197.3 6.5 %collective-permute-start.20 = (f32[4,2,18,1]{3,1,2,0:T(2,128)S(1)}, f32[4,2,18,1]{3,1,2,0:T(2,128)S(1)}, u32[]{:S(2)}, u32[]{:S(2)}) collective-permute-start(f32[4,2,18,1]{3,1,2,0:T(2,128)S(1)} %get-tuple-element.394), channel_id=1, source_target_pairs={{0,2},{1,3},{4,6},{5,7},{8,10},{9,11},{12,14},{13,15},{16,18},{17,... | collective-permute-start | bytes 1736 | tf_op jit(solution)/shard_map/ppermute | solution.py:27
  205.3 6.0 %collective-permute-start.23 = (f32[2,1,1,8,6,128]{5,3,0,4,2,1:T(8,128)S(1)}, f32[2,1,1,8,6,128]{5,3,0,4,2,1:T(8,128)S(1)}, u32[]{:S(2)}, u32[]{:S(2)}) collective-permute-start(f32[2,1,1,8,6,128]{5,3,0,4,2,1:T(8,128)S(1)} %maximum_bitcast_fusion.5), channel_id=1, source_target_pairs={{4,0},{8,4},{12,8},{5,1},{9,5},{13,9},{6,2},{10,6},{14,10},{7,3},{... | collective-permute-start | bytes 147464 | tf_op jit(solution)/shard_map/ppermute | solution.py:29
  206.6 6.3 %collective-permute-start.22 = (f32[2,1,1,8,6,128]{5,3,0,4,2,1:T(8,128)S(1)}, f32[2,1,1,8,6,128]{5,3,0,4,2,1:T(8,128)S(1)}, u32[]{:S(2)}, u32[]{:S(2)}) collective-permute-start(f32[2,1,1,8,6,128]{5,3,0,4,2,1:T(8,128)S(1)} %maximum_bitcast_fusion.5), channel_id=1, source_target_pairs={{0,4},{4,8},{8,12},{1,5},{5,9},{9,13},{2,6},{6,10},{10,14},{3,7},{... | collective-permute-start | bytes 147464 | tf_op jit(solution)/shard_map/ppermute | solution.py:27
  212.9 15.9 %collective-permute-start.25 = (f32[2,3,1,8,6,128]{5,3,0,4,2,1:T(8,128)S(1)}, f32[2,3,1,8,6,128]{5,3,0,4,2,1:T(8,128)S(1)}, u32[]{:S(2)}, u32[]{:S(2)}) collective-permute-start(f32[2,3,1,8,6,128]{5,3,0,4,2,1:T(8,128)S(1)} %pad_maximum_fusion.5), channel_id=1, source_target_pairs={{2,0},{3,1},{6,4},{7,5},{10,8},{11,9},{14,12},{15,13},{18,16},{19,... | collective-permute-start | bytes 442376 | tf_op jit(solution)/shard_map/ppermute | solution.py:29
  214.2 14.6 %collective-permute-start.24 = (f32[2,3,1,8,6,128]{5,3,0,4,2,1:T(8,128)S(1)}, f32[2,3,1,8,6,128]{5,3,0,4,2,1:T(8,128)S(1)}, u32[]{:S(2)}, u32[]{:S(2)}) collective-permute-start(f32[2,3,1,8,6,128]{5,3,0,4,2,1:T(8,128)S(1)} %pad_maximum_fusion.5), channel_id=1, source_target_pairs={{0,2},{1,3},{4,6},{5,7},{8,10},{9,11},{12,14},{13,15},{16,18},{17,... | collective-permute-start | bytes 442376 | tf_op jit(solution)/shard_map/ppermute | solution.py:27
  250.4 5.6 %collective-permute-start.26 = (f32[4,2,64]{2,1,0:T(2,128)S(1)}, f32[4,2,64]{2,1,0:T(2,128)S(1)}, u32[]{:S(2)}, u32[]{:S(2)}) collective-permute-start(f32[4,2,64]{2,1,0:T(2,128)S(1)} %bitcast.385), channel_id=1, source_target_pairs={{0,4},{4,8},{8,12},{1,5},{5,9},{9,13},{2,6},{6,10},{10,14},{3,7},{... | collective-permute-start | bytes 6152 | tf_op jit(solution)/shard_map/ppermute | solution.py:39
where the time goes:
time: 258 us; the launch traced here: 257 us
  other arithmetic  91.1 us (35%)
  starting transfers between devices  77.3 us (30%)
  blocking collectives  34.4 us (13%)
  waiting for transfers between devices  20.1 us (8%)
  local copies, waits for them, and re-layouts  16.5 us (6%)
  between operations  11.3 us (4%)
  loops' own time  5.87 us (2%)
    ppermute x12, starting transfers between devices, with_halo(): lax.ppermute(tail, axis, [(i, (i + 1) % count) for i in range(ends)])  49.9 us
    all_gather x3, blocking collectives, on_device(): lax.all_gather(moment_got, ('span', 'blade'), axis=1, tiled=True)  15.9 us
    ppermute x12, starting transfers between devices, with_halo(): lax.ppermute(head, axis, [((i + 1) % count, i) for i in range(ends)])  15.5 us
    sub x48, other arithmetic, near_velocity(): strengths[1][None, :] * separation[2]  14.4 us
    reduce_sum x48, other arithmetic, far_velocity(): return inv_four_pi * jnp.sum(values, axis=2)  13.4 us
    psum x1, blocking collectives, spread(): return lax.psum(jnp.where(mine, shard, jnp.zeros_like(shard)), axis)  13.3 us
    ppermute x3, starting transfers between devices, shifted(): lax.ppermute(value, axis, [(source, source + steps) for source in range(f...  11.9 us
    reduce_sum x48, other arithmetic, near_velocity(): dist_sq = jnp.sum(separation * separation, axis=0) + near_core  10.6 us
  transfers between devices with their start and end apart: 27, of which 14 were waited for; matrix products, arithmetic and copies ran while one was open for 15% of the time, Pallas kernels for 0%

commit v1 on v0

--- a/solution.py
+++ b/solution.py
@@ -9,6 +9,19 @@
 near_core = 0.0025
 far_core = 0.01
 inv_four_pi = 0.25 / math.pi
+
+
+def gather_around(x, axis, dim):
+    ways = lax.axis_size(axis)
+    up = [(d, (d + 1) % ways) for d in range(ways)]
+    down = [(d, (d - 1) % ways) for d in range(ways)]
+    earlier, later = ([x], [x])
+    for _ in range(ways // 2):
+        earlier.append(lax.ppermute(earlier[-1], axis, up))
+    for _ in range((ways - 1) // 2):
+        later.append(lax.ppermute(later[-1], axis, down))
+    line = jnp.concatenate([*earlier[::-1], *later[1:]], axis=dim)
+    return jnp.roll(line, (lax.axis_index(axis) - ways // 2) * x.shape[dim], axis=dim)
 
 
 def spread(shard, axis, root):
@@ -158,7 +171,7 @@
             spread(moment_local, "age", azimuth // az_dev),
             spread(trailing_local, "age", azimuth // az_dev),
         )
-        moment_all = lax.all_gather(moment_got, ("span", "blade"), axis=1, tiled=True)
+        moment_all = gather_around(moment_got, ("span", "blade"), 1)
         turn_frac = azimuth.astype(jnp.float32) / naz_total
         source_angle = 2.0 * math.pi * (turn_frac + column_frac)
         source_cos = jnp.cos(source_angle)

time: 258 us -> 245 us (0.950)
  blocking collectives: 34.4 us -> 19.3 us
  starting transfers between devices: 77.3 us -> 81.8 us
    all_gather x3 -> x0, blocking collectives: 15.9 us -> none  [on_device(): lax.all_gather(moment_got, ('span', 'blade'), axis=1, tiled=True)]
    ppermute x0 -> x9, starting transfers between devices: none -> 6.08 us  [the longest x3 3.3 us: gather_around(): later.append(lax.ppermute(later[-1], axis, down))]
  transfers between devices with their start and end apart: 27 -> 36, of which waited for: 14 -> 14; matrix products, arithmetic and copies ran while one was open for 15% -> 14% of each run, Pallas kernels for 0% -> 0%
where the time goes in v1:
time: 245 us; the launch traced here: 244 us
  other arithmetic  89.1 us (36%)
  starting transfers between devices  81.8 us (33%)
  waiting for transfers between devices  20.7 us (8%)
  blocking collectives  19.3 us (8%)
  local copies, waits for them, and re-layouts  15.1 us (6%)
  between operations  11.8 us (5%)
  loops' own time  5.87 us (2%)
    ppermute x12, starting transfers between devices, with_halo(): lax.ppermute(tail, axis, [(i, (i + 1) % count) for i in range(ends)])  48.1 us
    ppermute x12, starting transfers between devices, with_halo(): lax.ppermute(head, axis, [((i + 1) % count, i) for i in range(ends)])  15.5 us
    sub x48, other arithmetic, near_velocity(): strengths[1][None, :] * separation[2]  14.4 us
    psum x1, blocking collectives, spread(): return lax.psum(jnp.where(mine, shard, jnp.zeros_like(shard)), axis)  13.9 us
    reduce_sum x48, other arithmetic, far_velocity(): return inv_four_pi * jnp.sum(values, axis=2)  13.4 us
    ppermute x3, starting transfers between devices, shifted(): lax.ppermute(value, axis, [(source, source + steps) for source in range(f...  12.1 us
    ppermute x12, waiting for transfers between devices, with_halo(): lax.ppermute(head, axis, [((i + 1) % count, i) for i in range(ends)])  10.8 us
    reduce_sum x48, other arithmetic, near_velocity(): dist_sq = jnp.sum(separation * separation, axis=0) + near_core  10.6 us
  transfers between devices with their start and end apart: 36, of which 14 were waited for; matrix products, arithmetic and copies ran while one was open for 14% of the time, Pallas kernels for 0%

profile of v1, /device:TPU:0, one launch (start us, length us, event | category | flops | bytes accessed | tf_op | source)
XLA Modules:
  0.0 243.6 jit_solution(17921101156365543727)
XLA Ops:
  14.2 13.9 %all-reduce = (f32[3,128]{1,0:T(4,128)S(1)}, f32[1,2,64]{2,1,0:T(2,128)S(1)}, f32[3,128]{1,0:T(4,128)S(1)}, f32[1,2,64]{2,1,0:T(2,128)S(1)}, f32[3,128]{1,0:T(4,128)S(1)}, /*index=5*/f32[1,2,64]{2,1,0:T(2,128)S(1)}) all-reduce(f32[3,128]{1,0:T(4,128)S(1)} %select_n.386, ...), channel_id=1, replica_groups=mesh['groups'=2,'age'=4,'span'=2,'blade'=2] {'age'}, use_global_device_ids=true, to_apply=%region_5.6 | all-reduce | flops 1536 | bytes 12288 | tf_op jit(solution)/shard_map/psum | solution.py:29
  28.1 1.7 collective-permute-start.2
  36.6 5.4 %all_gather.3 = f32[3,512]{1,0:T(4,128)S(1)} all-gather(f32[3,128]{1,0:T(4,128)S(1)} %div.142), channel_id=1, replica_groups=mesh['groups'=2,'age'=4,'span'=2,'blade'=2] {'span','blade'}, dimensions={1}, use_global_device_ids=true | all-gather | bytes 7680 | tf_op jit(solution)/shard_map/all_gather | solution.py:159
  44.3 4.5 %collective-permute-start.5 = (f32[4,2,18,1]{3,1,2,0:T(2,128)S(1)}, f32[4,2,18,1]{3,1,2,0:T(2,128)S(1)}, u32[]{:S(2)}, u32[]{:S(2)}) collective-permute-start(f32[4,2,18,1]{3,1,2,0:T(2,128)S(1)} %get-tuple-element.399), channel_id=1, source_target_pairs={{0,2},{1,3},{4,6},{5,7},{8,10},{9,11},{12,14},{13,15},{16,18},{17,... | collective-permute-start | bytes 1736 | tf_op jit(solution)/shard_map/ppermute | solution.py:40
  53.9 4.9 %collective-permute-start.7 = (f32[2,1,1,8,6,128]{5,3,0,4,2,1:T(8,128)S(1)}, f32[2,1,1,8,6,128]{5,3,0,4,2,1:T(8,128)S(1)}, u32[]{:S(2)}, u32[]{:S(2)}) collective-permute-start(f32[2,1,1,8,6,128]{5,3,0,4,2,1:T(8,128)S(1)} %maximum_bitcast_fusion.3), channel_id=1, source_target_pairs={{0,4},{4,8},{8,12},{1,5},{5,9},{9,13},{2,6},{6,10},{10,14},{3,7},{... | collective-permute-start | bytes 147464 | tf_op jit(solution)/shard_map/ppermute | solution.py:40
  59.0 9.9 %while.60 = (s32[]{:T(128)}, f32[16,1,3,128]{3,2,1,0:T(4,128)S(1)}, f32[3,512]{1,0:T(4,128)S(1)}, f32[16,1,3,128]{3,2,1,0:T(4,128)S(1)}, f32[3,512]{1,0:T(4,128)S(1)}, /*index=5*/s32[]{:T(128)}) while((s32[]{:T(128)}, f32[16,1,3,128]{3,2,1,0:T(4,128)S(1)}, f32[3,512]{1,0:T(4,128)S(1)}, f32[16,1,3,128]{3,2,1,0:T(4,128)S(1)}, ...), condition=%wide.region_10.12_spmd, body=%wide.region_6.11_spmd.sunk | while | flops 2293762 | bytes 2133589 | solution.py:114
  68.9 1.5 collective-permute-start.14
  71.2 1.7 collective-permute-start.13
  74.2 4.6 %collective-permute-start.9 = (f32[2,3,1,8,6,128]{5,3,0,4,2,1:T(8,128)S(1)}, f32[2,3,1,8,6,128]{5,3,0,4,2,1:T(8,128)S(1)}, u32[]{:S(2)}, u32[]{:S(2)}) collective-permute-start(f32[2,3,1,8,6,128]{5,3,0,4,2,1:T(8,128)S(1)} %pad_maximum_fusion.3), channel_id=1, source_target_pairs={{0,2},{1,3},{4,6},{5,7},{8,10},{9,11},{12,14},{13,15},{16,18},{17,... | collective-permute-start | bytes 442376 | tf_op jit(solution)/shard_map/ppermute | solution.py:40
  79.0 1.6 collective-permute-done.10
  83.3 19.9 %while.61 = (s32[]{:T(128)}, f32[16,1,3,128]{3,2,1,0:T(4,128)S(1)}, f32[16,1,3,1024]{3,0,2,1:T(8,128)S(1)}, f32[16,1,3,128]{3,2,1,0:T(4,128)S(1)}, f32[16,1,3,1024]{3,0,2,1:T(8,128)S(1)}, /*index=5*/s32[]{:T(128)}) while((s32[]{:T(128)}, f32[16,1,3,128]{3,2,1,0:T(4,128)S(1)}, f32[16,1,3,1024]{3,0,2,1:T(8,128)S(1)}, ...), condition=%wide.region_14.16_spmd, body=%wide.region_11.15_spmd.sunk | while | flops 4587522 | bytes 8560217 | solution.py:114
  103.5 3.6 %collective-permute-start.11 = (f32[4,2,64]{2,1,0:T(2,128)S(1)}, f32[4,2,64]{2,1,0:T(2,128)S(1)}, u32[]{:S(2)}, u32[]{:S(2)}) collective-permute-start(f32[4,2,64]{2,1,0:T(2,128)S(1)} %get-tuple-element.404), channel_id=1, source_target_pairs={{0,4},{4,8},{8,12},{1,5},{5,9},{9,13},{2,6},{6,10},{10,14},{3,7},{... | collective-permute-start | bytes 6152 | tf_op jit(solution)/shard_map/ppermute | solution.py:52
  107.3 2.5 %collective-permute-start.15 = (f32[4,2,1,64]{3,1,0,2:T(2,128)S(1)}, f32[4,2,1,64]{3,1,0,2:T(2,128)S(1)}, u32[]{:S(2)}, u32[]{:S(2)}) collective-permute-start(f32[4,2,1,64]{3,1,0,2:T(2,128)S(1)} %get-tuple-element.403), channel_id=1, source_target_pairs={{0,4},{4,8},{8,12},{1,5},{5,9},{9,13},{2,6},{6,10},{10,14},{3,7},{... | collective-permute-start | bytes 6152 | tf_op jit(solution)/shard_map/ppermute | solution.py:40
  111.1 4.1 %collective-permute-done.16 = f32[4,2,1,64]{3,1,0,2:T(2,128)S(1)} collective-permute-done((f32[4,2,1,64]{3,1,0,2:T(2,128)S(1)}, f32[4,2,1,64]{3,1,0,2:T(2,128)S(1)}, u32[]{:S(2)}, u32[]{:S(2)}) %collective-permute-start.16) | collective-permute-done | bytes 2080 | tf_op jit(solution)/shard_map/ppermute | solution.py:42
  116.8 4.5 %collective-permute-start.17 = (f32[4,2,18,1]{3,1,0,2:T(2,128)S(1)}, f32[4,2,18,1]{3,1,0,2:T(2,128)S(1)}, u32[]{:S(2)}, u32[]{:S(2)}) collective-permute-start(f32[4,2,18,1]{3,1,0,2:T(2,128)S(1)} %get-tuple-element.397), channel_id=1, source_target_pairs={{0,2},{1,3},{4,6},{5,7},{8,10},{9,11},{12,14},{13,15},{16,18},{17,... | collective-permute-start | bytes 1736 | tf_op jit(solution)/shard_map/ppermute | solution.py:40
  121.7 1.6 collective-permute-done.17
  126.0 4.5 %collective-permute-start.19 = (f32[2,1,1,8,6,128]{5,3,0,4,2,1:T(8,128)S(1)}, f32[2,1,1,8,6,128]{5,3,0,4,2,1:T(8,128)S(1)}, u32[]{:S(2)}, u32[]{:S(2)}) collective-permute-start(f32[2,1,1,8,6,128]{5,3,0,4,2,1:T(8,128)S(1)} %maximum_bitcast_fusion.4), channel_id=1, source_target_pairs={{0,4},{4,8},{8,12},{1,5},{5,9},{9,13},{2,6},{6,10},{10,14},{3,7},{... | collective-permute-start | bytes 147464 | tf_op jit(solution)/shard_map/ppermute | solution.py:40
  130.7 1.6 collective-permute-done.19
  133.6 4.7 %collective-permute-start.21 = (f32[2,3,1,8,6,128]{5,3,0,4,2,1:T(8,128)S(1)}, f32[2,3,1,8,6,128]{5,3,0,4,2,1:T(8,128)S(1)}, u32[]{:S(2)}, u32[]{:S(2)}) collective-permute-start(f32[2,3,1,8,6,128]{5,3,0,4,2,1:T(8,128)S(1)} %pad_maximum_fusion.4), channel_id=1, source_target_pairs={{0,2},{1,3},{4,6},{5,7},{8,10},{9,11},{12,14},{13,15},{16,18},{17,... | collective-permute-start | bytes 442376 | tf_op jit(solution)/shard_map/ppermute | solution.py:40
  138.4 9.9 %while.62 = (s32[]{:T(128)}, f32[16,1,3,128]{3,2,1,0:T(4,128)S(1)}, f32[3,512]{1,0:T(4,128)S(1)}, f32[16,1,3,128]{3,2,1,0:T(4,128)S(1)}, f32[3,512]{1,0:T(4,128)S(1)}, /*index=5*/s32[]{:T(128)}) while((s32[]{:T(128)}, f32[16,1,3,128]{3,2,1,0:T(4,128)S(1)}, f32[3,512]{1,0:T(4,128)S(1)}, f32[16,1,3,128]{3,2,1,0:T(4,128)S(1)}, ...), condition=%wide.region_21.23_spmd, body=%wide.region_17.22_spmd.sunk | while | flops 2293762 | bytes 2133589 | solution.py:114
  149.9 19.9 %while.63 = (s32[]{:T(128)}, f32[16,1,3,128]{3,2,1,0:T(4,128)S(1)}, f32[16,1,3,1024]{3,0,2,1:T(8,128)S(1)}, f32[16,1,3,128]{3,2,1,0:T(4,128)S(1)}, f32[16,1,3,1024]{3,0,2,1:T(8,128)S(1)}, /*index=5*/s32[]{:T(128)}) while((s32[]{:T(128)}, f32[16,1,3,128]{3,2,1,0:T(4,128)S(1)}, f32[16,1,3,1024]{3,0,2,1:T(8,128)S(1)}, ...), condition=%wide.region_25.27_spmd, body=%wide.region_22.26_spmd.sunk | while | flops 4587522 | bytes 8560217 | solution.py:114
  170.1 4.2 %collective-permute-start.23 = (f32[4,2,64]{2,1,0:T(2,128)S(1)}, f32[4,2,64]{2,1,0:T(2,128)S(1)}, u32[]{:S(2)}, u32[]{:S(2)}) collective-permute-start(f32[4,2,64]{2,1,0:T(2,128)S(1)} %get-tuple-element.402), channel_id=1, source_target_pairs={{0,4},{4,8},{8,12},{1,5},{5,9},{9,13},{2,6},{6,10},{10,14},{3,7},{... | collective-permute-start | bytes 6152 | tf_op jit(solution)/shard_map/ppermute | solution.py:52
  174.4 2.8 %collective-permute-start.27 = (f32[4,2,1,64]{3,1,0,2:T(2,128)S(1)}, f32[4,2,1,64]{3,1,0,2:T(2,128)S(1)}, u32[]{:S(2)}, u32[]{:S(2)}) collective-permute-start(f32[4,2,1,64]{3,1,0,2:T(2,128)S(1)} %get-tuple-element.401), channel_id=1, source_target_pairs={{0,4},{4,8},{8,12},{1,5},{5,9},{9,13},{2,6},{6,10},{10,14},{3,7},{... | collective-permute-start | bytes 6152 | tf_op jit(solution)/shard_map/ppermute | solution.py:40
  178.6 4.2 %collective-permute-done.28 = f32[4,2,1,64]{3,1,2,0:T(2,128)S(1)} collective-permute-done((f32[4,2,1,64]{3,1,2,0:T(2,128)S(1)}, f32[4,2,1,64]{3,1,2,0:T(2,128)S(1)}, u32[]{:S(2)}, u32[]{:S(2)}) %collective-permute-start.28) | collective-permute-done | bytes 2080 | tf_op jit(solution)/shard_map/ppermute | solution.py:42
  184.2 4.5 %collective-permute-start.29 = (f32[4,2,18,1]{3,1,2,0:T(2,128)S(1)}, f32[4,2,18,1]{3,1,2,0:T(2,128)S(1)}, u32[]{:S(2)}, u32[]{:S(2)}) collective-permute-start(f32[4,2,18,1]{3,1,2,0:T(2,128)S(1)} %get-tuple-element.395), channel_id=1, source_target_pairs={{0,2},{1,3},{4,6},{5,7},{8,10},{9,11},{12,14},{13,15},{16,18},{17,... | collective-permute-start | bytes 1736 | tf_op jit(solution)/shard_map/ppermute | solution.py:40
  189.2 1.6 collective-permute-done.29
  193.5 4.5 %collective-permute-start.31 = (f32[2,1,1,8,6,128]{5,3,0,4,2,1:T(8,128)S(1)}, f32[2,1,1,8,6,128]{5,3,0,4,2,1:T(8,128)S(1)}, u32[]{:S(2)}, u32[]{:S(2)}) collective-permute-start(f32[2,1,1,8,6,128]{5,3,0,4,2,1:T(8,128)S(1)} %maximum_bitcast_fusion.5), channel_id=1, source_target_pairs={{0,4},{4,8},{8,12},{1,5},{5,9},{9,13},{2,6},{6,10},{10,14},{3,7},{... | collective-permute-start | bytes 147464 | tf_op jit(solution)/shard_map/ppermute | solution.py:40
  198.2 1.6 collective-permute-done.31
  201.1 4.6 %collective-permute-start.33 = (f32[2,3,1,8,6,128]{5,3,0,4,2,1:T(8,128)S(1)}, f32[2,3,1,8,6,128]{5,3,0,4,2,1:T(8,128)S(1)}, u32[]{:S(2)}, u32[]{:S(2)}) collective-permute-start(f32[2,3,1,8,6,128]{5,3,0,4,2,1:T(8,128)S(1)} %pad_maximum_fusion.5), channel_id=1, source_target_pairs={{0,2},{1,3},{4,6},{5,7},{8,10},{9,11},{12,14},{13,15},{16,18},{17,... | collective-permute-start | bytes 442376 | tf_op jit(solution)/shard_map/ppermute | solution.py:40
  205.7 9.9 %while.64 = (s32[]{:T(128)}, f32[16,1,3,128]{3,2,1,0:T(4,128)S(1)}, f32[3,512]{1,0:T(4,128)S(1)}, f32[16,1,3,128]{3,2,1,0:T(4,128)S(1)}, f32[3,512]{1,0:T(4,128)S(1)}, /*index=5*/s32[]{:T(128)}) while((s32[]{:T(128)}, f32[16,1,3,128]{3,2,1,0:T(4,128)S(1)}, f32[3,512]{1,0:T(4,128)S(1)}, f32[16,1,3,128]{3,2,1,0:T(4,128)S(1)}, ...), condition=%wide.region_32.34_spmd, body=%wide.region_28.33_spmd.sunk | while | flops 2293762 | bytes 2133589 | solution.py:114
  217.2 19.9 %while.65 = (s32[]{:T(128)}, f32[16,1,3,128]{3,2,1,0:T(4,128)S(1)}, f32[16,1,3,1024]{3,0,2,1:T(8,128)S(1)}, f32[16,1,3,128]{3,2,1,0:T(4,128)S(1)}, f32[16,1,3,1024]{3,0,2,1:T(8,128)S(1)}, /*index=5*/s32[]{:T(128)}) while((s32[]{:T(128)}, f32[16,1,3,128]{3,2,1,0:T(4,128)S(1)}, f32[16,1,3,1024]{3,0,2,1:T(8,128)S(1)}, ...), condition=%wide.region_36.38_spmd, body=%wide.region_33.37_spmd.sunk | while | flops 4587522 | bytes 8560217 | solution.py:114
  237.3 4.2 %collective-permute-start.35 = (f32[4,2,64]{2,1,0:T(2,128)S(1)}, f32[4,2,64]{2,1,0:T(2,128)S(1)}, u32[]{:S(2)}, u32[]{:S(2)}) collective-permute-start(f32[4,2,64]{2,1,0:T(2,128)S(1)} %bitcast.385), channel_id=1, source_target_pairs={{0,4},{4,8},{8,12},{1,5},{5,9},{9,13},{2,6},{6,10},{10,14},{3,7},{... | collective-permute-start | bytes 6152 | tf_op jit(solution)/shard_map/ppermute | solution.py:52
  (994 shorter events, 126.5 us)
Async XLA Ops:
  28.1 20.8 %collective-permute-start = (f32[3,128]{1,0:T(4,128)S(1)}, f32[3,128]{1,0:T(4,128)S(1)}, u32[]{:S(2)}, u32[]{:S(2)}) collective-permute-start(f32[3,128]{1,0:T(4,128)S(1)} %get-tuple-element.345), channel_id=1, source_target_pairs={{0,1},{1,2},{2,3},{3,0},{4,5},{5,6},{6,7},{7,4},{8,9},{9,10},{10,1... | collective-permute-start | bytes 4616 | tf_op jit(solution)/shard_map/ppermute | solution.py:20
  28.1 24.1 %collective-permute-start.2 = (f32[3,128]{1,0:T(4,128)S(1)}, f32[3,128]{1,0:T(4,128)S(1)}, u32[]{:S(2)}, u32[]{:S(2)}) collective-permute-start(f32[3,128]{1,0:T(4,128)S(1)} %get-tuple-element.345), channel_id=1, source_target_pairs={{0,3},{1,0},{2,1},{3,2},{4,7},{5,4},{6,5},{7,6},{8,11},{9,8},{10,9... | collective-permute-start | bytes 4616 | tf_op jit(solution)/shard_map/ppermute | solution.py:22
  31.2 11.6 %collective-permute-start.3 = (f32[4,2,1,64]{3,1,2,0:T(2,128)S(1)}, f32[4,2,1,64]{3,1,2,0:T(2,128)S(1)}, u32[]{:S(2)}, u32[]{:S(2)}) collective-permute-start(f32[4,2,1,64]{3,1,2,0:T(2,128)S(1)} %copy.303), channel_id=1, source_target_pairs={{0,4},{4,8},{8,12},{1,5},{5,9},{9,13},{2,6},{6,10},{10,14},{3,7},{... | collective-permute-start | bytes 6152 | tf_op jit(solution)/shard_map/ppermute | solution.py:40
  32.5 10.3 %collective-permute-start.4 = (f32[4,2,1,64]{3,1,2,0:T(2,128)S(1)}, f32[4,2,1,64]{3,1,2,0:T(2,128)S(1)}, u32[]{:S(2)}, u32[]{:S(2)}) collective-permute-start(f32[4,2,1,64]{3,1,2,0:T(2,128)S(1)} %copy.304), channel_id=1, source_target_pairs={{4,0},{8,4},{12,8},{5,1},{9,5},{13,9},{6,2},{10,6},{14,10},{7,3},{... | collective-permute-start | bytes 6152 | tf_op jit(solution)/shard_map/ppermute | solution.py:42
  33.8 35.0 %collective-permute-start.24 = (f32[3,128]{1,0:T(4,128)S(1)}, f32[3,128]{1,0:T(4,128)S(1)}, u32[]{:S(2)}, u32[]{:S(2)}) collective-permute-start(f32[3,128]{1,0:T(4,128)S(1)} %get-tuple-element.349), channel_id=1, source_target_pairs={{0,1},{1,2},{2,3},{3,0},{4,5},{5,6},{6,7},{7,4},{8,9},{9,10},{10,1... | collective-permute-start | bytes 4616 | tf_op jit(solution)/shard_map/ppermute | solution.py:20
  43.0 6.3 %collective-permute-start.6 = (f32[4,2,18,1]{3,1,2,0:T(2,128)S(1)}, f32[4,2,18,1]{3,1,2,0:T(2,128)S(1)}, u32[]{:S(2)}, u32[]{:S(2)}) collective-permute-start(f32[4,2,18,1]{3,1,2,0:T(2,128)S(1)} %get-tuple-element.400), channel_id=1, source_target_pairs={{2,0},{3,1},{6,4},{7,5},{10,8},{11,9},{14,12},{15,13},{18,16},{19,... | collective-permute-start | bytes 1736 | tf_op jit(solution)/shard_map/ppermute | solution.py:42
  44.3 6.5 %collective-permute-start.5 = (f32[4,2,18,1]{3,1,2,0:T(2,128)S(1)}, f32[4,2,18,1]{3,1,2,0:T(2,128)S(1)}, u32[]{:S(2)}, u32[]{:S(2)}) collective-permute-start(f32[4,2,18,1]{3,1,2,0:T(2,128)S(1)} %get-tuple-element.399), channel_id=1, source_target_pairs={{0,2},{1,3},{4,6},{5,7},{8,10},{9,11},{12,14},{13,15},{16,18},{17,... | collective-permute-start | bytes 1736 | tf_op jit(solution)/shard_map/ppermute | solution.py:40
  48.9 25.3 %collective-permute-start.26 = (f32[3,128]{1,0:T(4,128)S(1)}, f32[3,128]{1,0:T(4,128)S(1)}, u32[]{:S(2)}, u32[]{:S(2)}) collective-permute-start(f32[3,128]{1,0:T(4,128)S(1)} %get-tuple-element.349), channel_id=1, source_target_pairs={{0,3},{1,0},{2,1},{3,2},{4,7},{5,4},{6,5},{7,6},{8,11},{9,8},{10,9... | collective-permute-start | bytes 4616 | tf_op jit(solution)/shard_map/ppermute | solution.py:22
  49.3 21.1 %collective-permute-start.12 = (f32[3,128]{1,0:T(4,128)S(1)}, f32[3,128]{1,0:T(4,128)S(1)}, u32[]{:S(2)}, u32[]{:S(2)}) collective-permute-start(f32[3,128]{1,0:T(4,128)S(1)} %get-tuple-element.347), channel_id=1, source_target_pairs={{0,1},{1,2},{2,3},{3,0},{4,5},{5,6},{6,7},{7,4},{8,9},{9,10},{10,1... | collective-permute-start | bytes 4616 | tf_op jit(solution)/shard_map/ppermute | solution.py:20
  52.3 18.9 %collective-permute-start.8 = (f32[2,1,1,8,6,128]{5,3,0,4,2,1:T(8,128)S(1)}, f32[2,1,1,8,6,128]{5,3,0,4,2,1:T(8,128)S(1)}, u32[]{:S(2)}, u32[]{:S(2)}) collective-permute-start(f32[2,1,1,8,6,128]{5,3,0,4,2,1:T(8,128)S(1)} %maximum_bitcast_fusion.3), channel_id=1, source_target_pairs={{4,0},{8,4},{12,8},{5,1},{9,5},{13,9},{6,2},{10,6},{14,10},{7,3},{... | collective-permute-start | bytes 147464 | tf_op jit(solution)/shard_map/ppermute | solution.py:42
  53.9 19.0 %collective-permute-start.7 = (f32[2,1,1,8,6,128]{5,3,0,4,2,1:T(8,128)S(1)}, f32[2,1,1,8,6,128]{5,3,0,4,2,1:T(8,128)S(1)}, u32[]{:S(2)}, u32[]{:S(2)}) collective-permute-start(f32[2,1,1,8,6,128]{5,3,0,4,2,1:T(8,128)S(1)} %maximum_bitcast_fusion.3), channel_id=1, source_target_pairs={{0,4},{4,8},{8,12},{1,5},{5,9},{9,13},{2,6},{6,10},{10,14},{3,7},{... | collective-permute-start | bytes 147464 | tf_op jit(solution)/shard_map/ppermute | solution.py:40
  68.9 10.1 %collective-permute-start.14 = (f32[3,128]{1,0:T(4,128)S(1)}, f32[3,128]{1,0:T(4,128)S(1)}, u32[]{:S(2)}, u32[]{:S(2)}) collective-permute-start(f32[3,128]{1,0:T(4,128)S(1)} %get-tuple-element.347), channel_id=1, source_target_pairs={{0,3},{1,0},{2,1},{3,2},{4,7},{5,4},{6,5},{7,6},{8,11},{9,8},{10,9... | collective-permute-start | bytes 4616 | tf_op jit(solution)/shard_map/ppermute | solution.py:22
  70.4 8.4 %collective-permute-start.25 = (f32[3,128]{1,0:T(4,128)S(1)}, f32[3,128]{1,0:T(4,128)S(1)}, u32[]{:S(2)}, u32[]{:S(2)}) collective-permute-start(f32[3,128]{1,0:T(4,128)S(1)} %collective-permute-done.24), channel_id=1, source_target_pairs={{0,1},{1,2},{2,3},{3,0},{4,5},{5,6},{6,7},{7,4},{8,9},{9,10},{10,1... | collective-permute-start | bytes 4616 | tf_op jit(solution)/shard_map/ppermute | solution.py:20
  71.2 7.7 %collective-permute-start.13 = (f32[3,128]{1,0:T(4,128)S(1)}, f32[3,128]{1,0:T(4,128)S(1)}, u32[]{:S(2)}, u32[]{:S(2)}) collective-permute-start(f32[3,128]{1,0:T(4,128)S(1)} %collective-permute-done.12), channel_id=1, source_target_pairs={{0,1},{1,2},{2,3},{3,0},{4,5},{5,6},{6,7},{7,4},{8,9},{9,10},{10,1... | collective-permute-start | bytes 4616 | tf_op jit(solution)/shard_map/ppermute | solution.py:20
  72.9 7.7 %collective-permute-start.10 = (f32[2,3,1,8,6,128]{5,3,0,4,2,1:T(8,128)S(1)}, f32[2,3,1,8,6,128]{5,3,0,4,2,1:T(8,128)S(1)}, u32[]{:S(2)}, u32[]{:S(2)}) collective-permute-start(f32[2,3,1,8,6,128]{5,3,0,4,2,1:T(8,128)S(1)} %pad_maximum_fusion.3), channel_id=1, source_target_pairs={{2,0},{3,1},{6,4},{7,5},{10,8},{11,9},{14,12},{15,13},{18,16},{19,... | collective-permute-start | bytes 442376 | tf_op jit(solution)/shard_map/ppermute | solution.py:42
  74.2 7.6 %collective-permute-start.9 = (f32[2,3,1,8,6,128]{5,3,0,4,2,1:T(8,128)S(1)}, f32[2,3,1,8,6,128]{5,3,0,4,2,1:T(8,128)S(1)}, u32[]{:S(2)}, u32[]{:S(2)}) collective-permute-start(f32[2,3,1,8,6,128]{5,3,0,4,2,1:T(8,128)S(1)} %pad_maximum_fusion.3), channel_id=1, source_target_pairs={{0,2},{1,3},{4,6},{5,7},{8,10},{9,11},{12,14},{13,15},{16,18},{17,... | collective-permute-start | bytes 442376 | tf_op jit(solution)/shard_map/ppermute | solution.py:40
  103.5 6.3 %collective-permute-start.11 = (f32[4,2,64]{2,1,0:T(2,128)S(1)}, f32[4,2,64]{2,1,0:T(2,128)S(1)}, u32[]{:S(2)}, u32[]{:S(2)}) collective-permute-start(f32[4,2,64]{2,1,0:T(2,128)S(1)} %get-tuple-element.404), channel_id=1, source_target_pairs={{0,4},{4,8},{8,12},{1,5},{5,9},{9,13},{2,6},{6,10},{10,14},{3,7},{... | collective-permute-start | bytes 6152 | tf_op jit(solution)/shard_map/ppermute | solution.py:52
  115.5 6.2 %collective-permute-start.18 = (f32[4,2,18,1]{3,1,0,2:T(2,128)S(1)}, f32[4,2,18,1]{3,1,0,2:T(2,128)S(1)}, u32[]{:S(2)}, u32[]{:S(2)}) collective-permute-start(f32[4,2,18,1]{3,1,0,2:T(2,128)S(1)} %get-tuple-element.398), channel_id=1, source_target_pairs={{2,0},{3,1},{6,4},{7,5},{10,8},{11,9},{14,12},{15,13},{18,16},{19,... | collective-permute-start | bytes 1736 | tf_op jit(solution)/shard_map/ppermute | solution.py:42
  116.8 6.5 %collective-permute-start.17 = (f32[4,2,18,1]{3,1,0,2:T(2,128)S(1)}, f32[4,2,18,1]{3,1,0,2:T(2,128)S(1)}, u32[]{:S(2)}, u32[]{:S(2)}) collective-permute-start(f32[4,2,18,1]{3,1,0,2:T(2,128)S(1)} %get-tuple-element.397), channel_id=1, source_target_pairs={{0,2},{1,3},{4,6},{5,7},{8,10},{9,11},{12,14},{13,15},{16,18},{17,... | collective-permute-start | bytes 1736 | tf_op jit(solution)/shard_map/ppermute | solution.py:40
  124.7 6.0 %collective-permute-start.20 = (f32[2,1,1,8,6,128]{5,3,0,4,2,1:T(8,128)S(1)}, f32[2,1,1,8,6,128]{5,3,0,4,2,1:T(8,128)S(1)}, u32[]{:S(2)}, u32[]{:S(2)}) collective-permute-start(f32[2,1,1,8,6,128]{5,3,0,4,2,1:T(8,128)S(1)} %maximum_bitcast_fusion.4), channel_id=1, source_target_pairs={{4,0},{8,4},{12,8},{5,1},{9,5},{13,9},{6,2},{10,6},{14,10},{7,3},{... | collective-permute-start | bytes 147464 | tf_op jit(solution)/shard_map/ppermute | solution.py:42
  126.0 6.3 %collective-permute-start.19 = (f32[2,1,1,8,6,128]{5,3,0,4,2,1:T(8,128)S(1)}, f32[2,1,1,8,6,128]{5,3,0,4,2,1:T(8,128)S(1)}, u32[]{:S(2)}, u32[]{:S(2)}) collective-permute-start(f32[2,1,1,8,6,128]{5,3,0,4,2,1:T(8,128)S(1)} %maximum_bitcast_fusion.4), channel_id=1, source_target_pairs={{0,4},{4,8},{8,12},{1,5},{5,9},{9,13},{2,6},{6,10},{10,14},{3,7},{... | collective-permute-start | bytes 147464 | tf_op jit(solution)/shard_map/ppermute | solution.py:40
  132.3 16.1 %collective-permute-start.22 = (f32[2,3,1,8,6,128]{5,3,0,4,2,1:T(8,128)S(1)}, f32[2,3,1,8,6,128]{5,3,0,4,2,1:T(8,128)S(1)}, u32[]{:S(2)}, u32[]{:S(2)}) collective-permute-start(f32[2,3,1,8,6,128]{5,3,0,4,2,1:T(8,128)S(1)} %pad_maximum_fusion.4), channel_id=1, source_target_pairs={{2,0},{3,1},{6,4},{7,5},{10,8},{11,9},{14,12},{15,13},{18,16},{19,... | collective-permute-start | bytes 442376 | tf_op jit(solution)/shard_map/ppermute | solution.py:42
  133.6 14.8 %collective-permute-start.21 = (f32[2,3,1,8,6,128]{5,3,0,4,2,1:T(8,128)S(1)}, f32[2,3,1,8,6,128]{5,3,0,4,2,1:T(8,128)S(1)}, u32[]{:S(2)}, u32[]{:S(2)}) collective-permute-start(f32[2,3,1,8,6,128]{5,3,0,4,2,1:T(8,128)S(1)} %pad_maximum_fusion.4), channel_id=1, source_target_pairs={{0,2},{1,3},{4,6},{5,7},{8,10},{9,11},{12,14},{13,15},{16,18},{17,... | collective-permute-start | bytes 442376 | tf_op jit(solution)/shard_map/ppermute | solution.py:40
  170.1 7.1 %collective-permute-start.23 = (f32[4,2,64]{2,1,0:T(2,128)S(1)}, f32[4,2,64]{2,1,0:T(2,128)S(1)}, u32[]{:S(2)}, u32[]{:S(2)}) collective-permute-start(f32[4,2,64]{2,1,0:T(2,128)S(1)} %get-tuple-element.402), channel_id=1, source_target_pairs={{0,4},{4,8},{8,12},{1,5},{5,9},{9,13},{2,6},{6,10},{10,14},{3,7},{... | collective-permute-start | bytes 6152 | tf_op jit(solution)/shard_map/ppermute | solution.py:52
  177.2 5.5 %collective-permute-start.28 = (f32[4,2,1,64]{3,1,2,0:T(2,128)S(1)}, f32[4,2,1,64]{3,1,2,0:T(2,128)S(1)}, u32[]{:S(2)}, u32[]{:S(2)}) collective-permute-start(f32[4,2,1,64]{3,1,2,0:T(2,128)S(1)} %fusion.110), channel_id=1, source_target_pairs={{4,0},{8,4},{12,8},{5,1},{9,5},{13,9},{6,2},{10,6},{14,10},{7,3},{... | collective-permute-start | bytes 6152 | tf_op jit(solution)/shard_map/ppermute | solution.py:42
  182.9 6.2 %collective-permute-start.30 = (f32[4,2,18,1]{3,1,2,0:T(2,128)S(1)}, f32[4,2,18,1]{3,1,2,0:T(2,128)S(1)}, u32[]{:S(2)}, u32[]{:S(2)}) collective-permute-start(f32[4,2,18,1]{3,1,2,0:T(2,128)S(1)} %get-tuple-element.396), channel_id=1, source_target_pairs={{2,0},{3,1},{6,4},{7,5},{10,8},{11,9},{14,12},{15,13},{18,16},{19,... | collective-permute-start | bytes 1736 | tf_op jit(solution)/shard_map/ppermute | solution.py:42
  184.2 6.5 %collective-permute-start.29 = (f32[4,2,18,1]{3,1,2,0:T(2,128)S(1)}, f32[4,2,18,1]{3,1,2,0:T(2,128)S(1)}, u32[]{:S(2)}, u32[]{:S(2)}) collective-permute-start(f32[4,2,18,1]{3,1,2,0:T(2,128)S(1)} %get-tuple-element.395), channel_id=1, source_target_pairs={{0,2},{1,3},{4,6},{5,7},{8,10},{9,11},{12,14},{13,15},{16,18},{17,... | collective-permute-start | bytes 1736 | tf_op jit(solution)/shard_map/ppermute | solution.py:40
  192.2 6.0 %collective-permute-start.32 = (f32[2,1,1,8,6,128]{5,3,0,4,2,1:T(8,128)S(1)}, f32[2,1,1,8,6,128]{5,3,0,4,2,1:T(8,128)S(1)}, u32[]{:S(2)}, u32[]{:S(2)}) collective-permute-start(f32[2,1,1,8,6,128]{5,3,0,4,2,1:T(8,128)S(1)} %maximum_bitcast_fusion.5), channel_id=1, source_target_pairs={{4,0},{8,4},{12,8},{5,1},{9,5},{13,9},{6,2},{10,6},{14,10},{7,3},{... | collective-permute-start | bytes 147464 | tf_op jit(solution)/shard_map/ppermute | solution.py:42
  193.5 6.3 %collective-permute-start.31 = (f32[2,1,1,8,6,128]{5,3,0,4,2,1:T(8,128)S(1)}, f32[2,1,1,8,6,128]{5,3,0,4,2,1:T(8,128)S(1)}, u32[]{:S(2)}, u32[]{:S(2)}) collective-permute-start(f32[2,1,1,8,6,128]{5,3,0,4,2,1:T(8,128)S(1)} %maximum_bitcast_fusion.5), channel_id=1, source_target_pairs={{0,4},{4,8},{8,12},{1,5},{5,9},{9,13},{2,6},{6,10},{10,14},{3,7},{... | collective-permute-start | bytes 147464 | tf_op jit(solution)/shard_map/ppermute | solution.py:40
  199.8 15.9 %collective-permute-start.34 = (f32[2,3,1,8,6,128]{5,3,0,4,2,1:T(8,128)S(1)}, f32[2,3,1,8,6,128]{5,3,0,4,2,1:T(8,128)S(1)}, u32[]{:S(2)}, u32[]{:S(2)}) collective-permute-start(f32[2,3,1,8,6,128]{5,3,0,4,2,1:T(8,128)S(1)} %pad_maximum_fusion.5), channel_id=1, source_target_pairs={{2,0},{3,1},{6,4},{7,5},{10,8},{11,9},{14,12},{15,13},{18,16},{19,... | collective-permute-start | bytes 442376 | tf_op jit(solution)/shard_map/ppermute | solution.py:42
  201.1 14.6 %collective-permute-start.33 = (f32[2,3,1,8,6,128]{5,3,0,4,2,1:T(8,128)S(1)}, f32[2,3,1,8,6,128]{5,3,0,4,2,1:T(8,128)S(1)}, u32[]{:S(2)}, u32[]{:S(2)}) collective-permute-start(f32[2,3,1,8,6,128]{5,3,0,4,2,1:T(8,128)S(1)} %pad_maximum_fusion.5), channel_id=1, source_target_pairs={{0,2},{1,3},{4,6},{5,7},{8,10},{9,11},{12,14},{13,15},{16,18},{17,... | collective-permute-start | bytes 442376 | tf_op jit(solution)/shard_map/ppermute | solution.py:40
  237.3 5.6 %collective-permute-start.35 = (f32[4,2,64]{2,1,0:T(2,128)S(1)}, f32[4,2,64]{2,1,0:T(2,128)S(1)}, u32[]{:S(2)}, u32[]{:S(2)}) collective-permute-start(f32[4,2,64]{2,1,0:T(2,128)S(1)} %bitcast.385), channel_id=1, source_target_pairs={{0,4},{4,8},{8,12},{1,5},{5,9},{9,13},{2,6},{6,10},{10,14},{3,7},{... | collective-permute-start | bytes 6152 | tf_op jit(solution)/shard_map/ppermute | solution.py:52
  (9 other events, 103.1 us)
